TPU v7x, 32 devices: a whole 2x2x4 slice. The times are simulated.
32 devices in a mesh: pole: 2 (over x), row: 8 (over z, y), col: 2 (over core).
Axes of the slice: x: 2, y: 2, z: 4, core: 2. Of those that a mesh axis runs over, the one named last changes fastest.
Arguments:
- inverse: float32 [16, 2, 256, 256], P(('pole', 'row'), 'col'), parts along dimension 0, as said below
- panel: float32 [16, 2, 64, 1024], P(('pole', 'row'), 'col'), parts along dimension 0, may hold values from -0.25 to 0.25
- pattern: int32 [4, 4], replicated, may hold values 0 or 1
- dinv: float32 [8, 256, 256], P('pole', 'row', 'col'), parts along dimension 0, may hold values from -6 to 6
Outputs:
- off_diagonal: float32 [16, 2, 64, 1024], P(('pole', 'row'), 'col'), parts along dimension 0
- diagonal: float32 [8, 256, 256], P('pole', 'row', 'col'), parts along dimension 0
There are 2 independent parts, one for each index of `pole`. A program takes and returns all parts, laid end to end along the dimension named above; an argument that names none is the same for every part. Nothing has to cross between parts.
Inputs may be any that keep to these rules, and one draw needn't show every extreme that they name: inverse, read as the 1024 x 1024 matrix A of the first step, is symmetric.
All inputs are finite; a program needn't handle non-finite values.
Results may differ from a plain program's by a relative error of at most 0.000078.
Values sent between devices are 32-bit elements; how exact they have to be, the bound alone decides.
A program may use at most 64 MiB of HBM per device.

v0:
```python
import jax
import jax.numpy as jnp
from jax import lax
from jax.sharding import PartitionSpec as P


def swapped(value, axis, apart):
    mask = 2**apart
    pairs = [(source, source ^ mask) for source in range(lax.axis_size(axis))]
    return lax.ppermute(value, axis, pairs)


def group_flip(current, position, col_bits):
    if position < col_bits:
        return swapped(current, "col", position)
    return swapped(current, "row", position - col_bits)


def cross_flip(current, position, col_bits):
    if position < col_bits:
        return swapped(current, "col", position)
    return swapped(current, "row", position - col_bits)


def bit_at(device_at, position):
    return device_at >> position & 1


def collect(current, positions, device_at, col_bits):
    for position in positions:
        partner = group_flip(current, position, col_bits)
        upper_half = bit_at(device_at, position) == 1
        current = jnp.where(
            upper_half,
            jnp.concatenate([partner, current], 0),
            jnp.concatenate([current, partner], 0),
        )
    return current


def reduce_split(current, positions, device_at, col_bits):
    for position in positions:
        halfway = current.shape[0] // 2
        mine_bit = bit_at(device_at, position)
        kept_half = lax.dynamic_slice_in_dim(current, mine_bit * halfway, halfway, 0)
        sent_half = lax.dynamic_slice_in_dim(current, (1 - mine_bit) * halfway, halfway, 0)
        current = kept_half + group_flip(sent_half, position, col_bits)
    return current


def relabel(current, targets, device_at, col_bits):
    mapping = list(range(len(targets)))
    for column in range(len(targets)):
        if mapping[column] != targets[column]:
            lead_bit = mapping[column]
            other_bit = targets[column]
            shifted = cross_flip(cross_flip(current, lead_bit, col_bits), other_bit, col_bits)
            unequal = bit_at(device_at, lead_bit) != bit_at(device_at, other_bit)
            current = jnp.where(unequal, shifted, current)
            mapping = [
                other_bit if element == lead_bit else lead_bit if element == other_bit else element
                for element in mapping
            ]
    return current


def body(inverse, panel, pattern, dinv):
    n_row = lax.axis_size("row")
    n_col = lax.axis_size("col")
    device_at = lax.axis_index("row") * n_col + lax.axis_index("col")
    grid_rows = min(8, n_row // 2)
    grid_cols = n_row * n_col // grid_rows
    col_bits = n_col.bit_length() - 1
    total_bits = (n_row * n_col).bit_length() - 1
    high_bits = grid_rows.bit_length() - 1
    side_bits = total_bits - high_bits
    grid_row = device_at // grid_cols
    grid_col = device_at % grid_cols
    rows_dev, col_count = (panel.shape[2], panel.shape[3])
    nblocks, sup_count = pattern.shape
    sup_width = col_count // sup_count
    first_row = (grid_col * grid_rows + grid_row) * rows_dev
    global_rows = first_row + jnp.arange(rows_dev, dtype=jnp.int32)
    onehot = (
        global_rows[:, None] // sup_width == jnp.arange(nblocks, dtype=jnp.int32)[None, :]
    ).astype(jnp.float32)
    keep_sup = jnp.dot(onehot, pattern.astype(jnp.float32), precision=lax.Precision.HIGHEST)
    keep_piece = jnp.broadcast_to(keep_sup[:, :, None], (rows_dev, sup_count, sup_width)).reshape(
        rows_dev, col_count
    )
    lhat_piece = panel.reshape(rows_dev, col_count) * keep_piece
    inverse_block = inverse.reshape(inverse.shape[2], inverse.shape[3])
    gathered = collect(lhat_piece, list(range(side_bits, total_bits)), device_at, col_bits)
    partial_sum = jnp.dot(
        inverse_block, gathered, precision=lax.Precision.HIGHEST, preferred_element_type=jnp.float32
    )
    row_piece = reduce_split(partial_sum, list(range(side_bits - 1, -1, -1)), device_at, col_bits)
    backward = [(bit_slot + side_bits) % total_bits for bit_slot in range(total_bits)]
    product_piece = relabel(row_piece, backward, device_at, col_bits)
    diag_terms = jnp.einsum(
        "rkw,rkv->kwv",
        lhat_piece.reshape(rows_dev, sup_count, sup_width),
        product_piece.reshape(rows_dev, sup_count, sup_width),
        precision=lax.Precision.HIGHEST,
    )
    arranged = diag_terms.reshape(sup_count, n_row, sup_width // n_row, n_col, sup_width // n_col)
    arranged = arranged.transpose(1, 3, 0, 2, 4).reshape(
        n_row * n_col, sup_count, sup_width // n_row, sup_width // n_col
    )
    diagonal = dinv + lax.psum_scatter(arranged, ("row", "col"), scatter_dimension=0, tiled=True)[0]
    off_diagonal = (-(product_piece * keep_piece)).reshape(panel.shape)
    return (off_diagonal, diagonal)


def solution(mesh):
    return jax.shard_map(
        body,
        mesh=mesh,
        in_specs=(
            P(("pole", "row"), "col", None, None),
            P(("pole", "row"), "col", None, None),
            P(),
            P("pole", "row", "col"),
        ),
        out_specs=(P(("pole", "row"), "col", None, None), P("pole", "row", "col")),
        check_vma=False,
    )
```

profile of v0, /device:TPU:0, one launch (start us, length us, event | category | flops | bytes accessed | tf_op | source)
XLA Modules:
  0.0 162.1 jit_solution(4960452260585040367)
XLA Ops:
  7.2 0.0 copy-start
  7.2 0.0 reduce-scatter.2.cloned.1.call-start
  7.2 0.0 copy-start.3
  7.3 0.7 copy-done.3
  7.9 0.2 fusion.12
  8.1 0.1 copy.10
  8.2 0.2 broadcast_in_dim.2.clone
  8.4 0.0 copy-start.1
  8.5 0.9 copy-done.1
  9.4 3.1 %collective-permute-start = (f32[64,1024]{1,0:T(8,128)S(1)}, f32[64,1024]{1,0:T(8,128)S(1)}, u32[]{:S(2)}, u32[]{:S(2)}) collective-permute-start(f32[64,1024]{1,0:T(8,128)S(1)} %bitcast_multiply_fusion), channel_id=1, source_target_pairs={{0,4},{2,6},{4,0},{6,2},{8,12},{10,14},{12,8},{14,10},{1,5},{3,7},... | collective-permute-start | bytes 786440 | tf_op jit(solution)/shard_map/ppermute | solution.py:10
  12.5 6.3 %collective-permute-done = f32[64,1024]{1,0:T(8,128)S(1)} collective-permute-done((f32[64,1024]{1,0:T(8,128)S(1)}, f32[64,1024]{1,0:T(8,128)S(1)}, u32[]{:S(2)}, u32[]{:S(2)}) %collective-permute-start) | collective-permute-done | bytes 262176 | tf_op jit(solution)/shard_map/ppermute | solution.py:10
  18.8 2.8 %collective-permute-start.1 = (f32[128,1024]{1,0:T(8,128)S(1)}, f32[128,1024]{1,0:T(8,128)S(1)}, u32[]{:S(2)}, u32[]{:S(2)}) collective-permute-start(f32[128,1024]{1,0:T(8,128)S(1)} %maximum_select_fusion.2), channel_id=1, source_target_pairs={{0,8},{2,10},{4,12},{6,14},{8,0},{10,2},{12,4},{14,6},{1,9},{3,11}... | collective-permute-start | bytes 1572872 | tf_op jit(solution)/shard_map/ppermute | solution.py:10
  21.6 22.5 %collective-permute-done.1 = f32[128,1024]{1,0:T(8,128)S(1)} collective-permute-done((f32[128,1024]{1,0:T(8,128)S(1)}, f32[128,1024]{1,0:T(8,128)S(1)}, u32[]{:S(2)}, u32[]{:S(2)}) %collective-permute-start.1) | collective-permute-done | bytes 524320 | tf_op jit(solution)/shard_map/ppermute | solution.py:10
  44.1 0.0 copy-done
  44.1 1.1 fusion
  45.3 1.4 collective-permute-start.2
  46.8 11.6 %collective-permute-done.2 = f32[128,1024]{1,0:T(8,128)S(1)} collective-permute-done((f32[128,1024]{1,0:T(8,128)S(1)}, f32[128,1024]{1,0:T(8,128)S(1)}, u32[]{:S(2)}, u32[]{:S(2)}) %collective-permute-start.2) | collective-permute-done | bytes 524320 | tf_op jit(solution)/shard_map/ppermute | solution.py:10
  58.3 0.1 bitcast_add_fusion
  58.4 0.1 collective-permute-start.3
  58.5 1.5 collective-permute-done.3
  60.1 0.2 collective-permute-start.4
  60.3 1.4 collective-permute-done.4
  61.7 1.4 collective-permute-start.5
  63.1 6.9 %collective-permute-done.5 = f32[64,1024]{1,0:T(8,128)S(1)} collective-permute-done((f32[64,1024]{1,0:T(8,128)S(1)}, f32[64,1024]{1,0:T(8,128)S(1)}, u32[]{:S(2)}, u32[]{:S(2)}) %collective-permute-start.5) | collective-permute-done | bytes 262176 | tf_op jit(solution)/shard_map/ppermute | solution.py:10
  70.1 1.3 collective-permute-start.6
  71.3 6.3 %collective-permute-done.6 = f32[64,1024]{1,0:T(8,128)S(1)} collective-permute-done((f32[64,1024]{1,0:T(8,128)S(1)}, f32[64,1024]{1,0:T(8,128)S(1)}, u32[]{:S(2)}, u32[]{:S(2)}) %collective-permute-start.6) | collective-permute-done | bytes 262176 | tf_op jit(solution)/shard_map/ppermute | solution.py:10
  77.6 3.4 %collective-permute-start.7 = (f32[64,1024]{1,0:T(8,128)S(1)}, f32[64,1024]{1,0:T(8,128)S(1)}, u32[]{:S(2)}, u32[]{:S(2)}) collective-permute-start(f32[64,1024]{1,0:T(8,128)S(1)} %collective-permute-done.6), channel_id=1, source_target_pairs={{0,8},{2,10},{4,12},{6,14},{8,0},{10,2},{12,4},{14,6},{1,9},{3,11}... | collective-permute-start | bytes 786440 | tf_op jit(solution)/shard_map/ppermute | solution.py:10
  81.0 0.1 reshape.71
  81.2 10.7 %collective-permute-done.7 = f32[64,1024]{1,0:T(8,128)S(1)} collective-permute-done((f32[64,1024]{1,0:T(8,128)S(1)}, f32[64,1024]{1,0:T(8,128)S(1)}, u32[]{:S(2)}, u32[]{:S(2)}) %collective-permute-start.7) | collective-permute-done | bytes 262176 | tf_op jit(solution)/shard_map/ppermute | solution.py:10
  91.8 0.8 negate_bitcast_fusion
  92.6 1.2 fusion.7
  93.8 0.5 reshape.73
  94.3 1.1 copy.9
  95.4 0.0 copy-start.2
  95.4 0.0 reduce-scatter.2.cloned.1.call-update
  95.5 58.4 %reduce-scatter.2.cloned.1.call-done = f32[1,4,32,128]{3,2,1,0:T(8,128)} async-done(((f32[16,4,32,128]{3,2,1,0:T(8,128)}), f32[1,4,32,128]{3,2,1,0:T(8,128)}) %reduce-scatter.2.cloned.1.call-update) | async-done | bytes 65552 | tf_op jit(solution)/shard_map/reduce_scatter | solution.py:110
  153.8 0.0 copy-done.2
  153.8 1.5 bitcast_add_fusion.1
  (8 shorter events, 0.3 us)
Async XLA Ops:
  7.2 37.0 %copy-start = (f32[1,1,256,256]{3,2,1,0:T(8,128)S(1)}, f32[1,1,256,256]{3,2,1,0:T(8,128)}, u32[]{:S(2)}) copy-start(f32[1,1,256,256]{3,2,1,0:T(8,128)} %param.4) | copy-start | bytes 786436
  7.2 146.6 %reduce-scatter.2.cloned.1.call-start = ((), (), s32[]{:S(2)}) async-start(), calls=%async_computation.1 | async-start | bytes 1114112 | tf_op jit(solution)/shard_map/reduce_scatter | solution.py:110
  7.2 0.7 copy-start.3
  8.4 1.0 copy-start.1
  9.4 9.4 %collective-permute-start = (f32[64,1024]{1,0:T(8,128)S(1)}, f32[64,1024]{1,0:T(8,128)S(1)}, u32[]{:S(2)}, u32[]{:S(2)}) collective-permute-start(f32[64,1024]{1,0:T(8,128)S(1)} %bitcast_multiply_fusion), channel_id=1, source_target_pairs={{0,4},{2,6},{4,0},{6,2},{8,12},{10,14},{12,8},{14,10},{1,5},{3,7},... | collective-permute-start | bytes 786440 | tf_op jit(solution)/shard_map/ppermute | solution.py:10
  18.8 25.3 %collective-permute-start.1 = (f32[128,1024]{1,0:T(8,128)S(1)}, f32[128,1024]{1,0:T(8,128)S(1)}, u32[]{:S(2)}, u32[]{:S(2)}) collective-permute-start(f32[128,1024]{1,0:T(8,128)S(1)} %maximum_select_fusion.2), channel_id=1, source_target_pairs={{0,8},{2,10},{4,12},{6,14},{8,0},{10,2},{12,4},{14,6},{1,9},{3,11}... | collective-permute-start | bytes 1572872 | tf_op jit(solution)/shard_map/ppermute | solution.py:10
  45.3 13.0 %collective-permute-start.2 = (f32[128,1024]{1,0:T(8,128)S(1)}, f32[128,1024]{1,0:T(8,128)S(1)}, u32[]{:S(2)}, u32[]{:S(2)}) collective-permute-start(f32[128,1024]{1,0:T(8,128)S(1)} %dynamic-slice_bitcast_fusion), channel_id=1, source_target_pairs={{0,2},{2,0},{4,6},{6,4},{8,10},{10,8},{12,14},{14,12},{1,3},{3,1},... | collective-permute-start | bytes 1572872 | tf_op jit(solution)/shard_map/ppermute | solution.py:10
  58.4 1.6 collective-permute-start.3
  60.1 1.6 collective-permute-start.4
  61.7 8.3 %collective-permute-start.5 = (f32[64,1024]{1,0:T(8,128)S(1)}, f32[64,1024]{1,0:T(8,128)S(1)}, u32[]{:S(2)}, u32[]{:S(2)}) collective-permute-start(f32[64,1024]{1,0:T(8,128)S(1)} %collective-permute-done.4), channel_id=1, source_target_pairs={{0,4},{2,6},{4,0},{6,2},{8,12},{10,14},{12,8},{14,10},{1,5},{3,7},... | collective-permute-start | bytes 786440 | tf_op jit(solution)/shard_map/ppermute | solution.py:10
  70.1 7.6 %collective-permute-start.6 = (f32[64,1024]{1,0:T(8,128)S(1)}, f32[64,1024]{1,0:T(8,128)S(1)}, u32[]{:S(2)}, u32[]{:S(2)}) collective-permute-start(f32[64,1024]{1,0:T(8,128)S(1)} %broadcast_select_fusion), channel_id=1, source_target_pairs={{0,2},{2,0},{4,6},{6,4},{8,10},{10,8},{12,14},{14,12},{1,3},{3,1},... | collective-permute-start | bytes 786440 | tf_op jit(solution)/shard_map/ppermute | solution.py:10
  77.6 14.2 %collective-permute-start.7 = (f32[64,1024]{1,0:T(8,128)S(1)}, f32[64,1024]{1,0:T(8,128)S(1)}, u32[]{:S(2)}, u32[]{:S(2)}) collective-permute-start(f32[64,1024]{1,0:T(8,128)S(1)} %collective-permute-done.6), channel_id=1, source_target_pairs={{0,8},{2,10},{4,12},{6,14},{8,0},{10,2},{12,4},{14,6},{1,9},{3,11}... | collective-permute-start | bytes 786440 | tf_op jit(solution)/shard_map/ppermute | solution.py:10
  95.4 58.4 %copy-start.2 = (f32[4,32,128]{2,1,0:T(8,128)S(1)}, f32[4,32,128]{2,1,0:T(8,128)}, u32[]{:S(2)}) copy-start(f32[4,32,128]{2,1,0:T(8,128)} %param.7) | copy-start | bytes 196612
Sparse Core Ops, SparseCore 0:
  95.6 58.1 reduce-scatter.1
where the time goes:
time: 162 us
  waiting for transfers between devices  126 us (78%)
  between operations  14.2 us (9%)
  starting transfers between devices  13.8 us (9%)
  local copies, waits for them, and re-layouts  3.73 us (2%)
  matrix products  2.47 us (2%)
  other arithmetic  2.45 us (2%)
    ppermute x8, waiting for transfers between devices, swapped(): return lax.ppermute(value, axis, pairs)  67.2 us
    reduce_scatter x1, waiting for transfers between devices, body(): lax.psum_scatter(arranged, ('row', 'col'), scatter_dimension=0, tiled=True)  58.4 us
    ppermute x8, starting transfers between devices, swapped(): return lax.ppermute(value, axis, pairs)  13.7 us
  transfers between devices with their start and end apart: 9, of which 9 were waited for; matrix products, arithmetic and copies ran while one was open for 0% of the time, Pallas kernels for 0%

commit v1 on v0

--- a/solution.py
+++ b/solution.py
@@ -1,6 +1,8 @@
 import jax
 import jax.numpy as jnp
 from jax import lax
+from jax.experimental import pallas as pl
+from jax.experimental.pallas import tpu as pltpu
 from jax.sharding import PartitionSpec as P
 
 
@@ -64,7 +66,7 @@
     return current
 
 
-def body(inverse, panel, pattern, dinv):
+def general_body(inverse, panel, pattern, dinv):
     n_row = lax.axis_size("row")
     n_col = lax.axis_size("col")
     device_at = lax.axis_index("row") * n_col + lax.axis_index("col")
@@ -112,6 +114,269 @@
     return (off_diagonal, diagonal)
 
 
+MESH = pl.DeviceIdType.MESH
+HIGHEST = lax.Precision.HIGHEST
+GRID = 4
+
+ROUTES = {
+    (0, 0): ([(1, 0, 0)], [], [(1, 0, 2)], [(1, 0, 3)]),
+    (0, 1): ([(0, 0, 1)], [], [(0, 2, 1)], [(0, 3, 1)]),
+    (0, 2): ([(0, 0, 2)], [], [(0, 3, 2)], []),
+    (0, 3): ([(0, 0, 3)], [], [], []),
+    (1, 0): ([(1, 1, 0)], [(2, 0, 0)], [(1, 2, 0)], [(1, 3, 0)]),
+    (1, 1): ([(0, 1, 1), (2, 1, 1)], [(2, 1, 0)], [(0, 1, 2)], [(0, 1, 3)]),
+    (1, 2): ([(1, 1, 2)], [(0, 2, 2)], [(0, 2, 3), (1, 3, 2)], []),
+    (1, 3): ([(1, 1, 3)], [(0, 3, 3)], [], []),
+}
+
+
+def numbered(routes):
+    count = 0
+    out = []
+    for targets in routes:
+        out.append([(count + n,) + t for n, t in enumerate(targets)])
+        count += len(targets)
+    return out
+
+
+def kernel(pattern_ref, a_ref, p_ref, dinv_ref, off_ref, diag_ref,
+           abuf, pbuf, acc, stage, dpart, dbuf, ebuf, dfin,
+           a_send, a_recv, p_send, p_recv, f_send, g_send, o_send, o_recv,
+           d_send, d_recv, e_send, e_recv):
+    width = a_ref.shape[0]
+    sub = p_ref.shape[0]
+    half_u, half_v = dinv_ref.shape[1], dinv_ref.shape[2]
+    pole = lax.axis_index("pole")
+    row = lax.axis_index("row")
+    c = lax.axis_index("col")
+    z = row // 2
+    y = row % 2
+    q = 2 * y + c
+    mirror = z // 2
+
+    def flip(v):
+        return v + mirror * (GRID - 1 - 2 * v)
+
+    zf, qf = flip(z), flip(q)
+
+    def dev(zt, qt):
+        return (pole, zt * 2 + qt // 2, qt % 2)
+
+    def copy_to(src, dst, send, recv, where):
+        return pltpu.make_async_remote_copy(
+            src_ref=src, dst_ref=dst, send_sem=send, recv_sem=recv,
+            device_id=where, device_id_type=MESH)
+
+    barrier = pltpu.get_barrier_semaphore()
+    me = z * GRID + q
+    for d in range(1, GRID * GRID):
+        other = (me + d) % (GRID * GRID)
+        pl.semaphore_signal(barrier, inc=1, device_id=dev(other // GRID, other % GRID), device_id_type=MESH)
+    pl.semaphore_wait(barrier, GRID * GRID - 1)
+
+    core_mate = q + 1 - 2 * c
+    across = q + 2 - 4 * y
+
+    def cols(k):
+        return pl.ds(pl.multiple_of(k * width, width), width)
+
+    def part(block, r):
+        return pl.ds(pl.multiple_of(block * width + r * sub, sub), sub)
+
+    z_copies = []
+    for d in (1, 3, 2):
+        zt = (z + d) % GRID
+        cp = copy_to(p_ref.at[:, cols(zt)], pbuf.at[part(q, z), :], p_send.at[d], p_recv.at[q * GRID + z], dev(zt, q))
+        cp.start()
+        z_copies.append(cp)
+
+    def a_copy(src, n, tz, tq, slot):
+        return copy_to(src, abuf.at[flip(slot)], a_send.at[n], a_recv.at[flip(slot)], dev(flip(tz), flip(tq)))
+
+    def a_pass(step, src):
+        for (cz, cq), routes in ROUTES.items():
+            targets = numbered(routes)[step]
+            if targets:
+                @pl.when((zf == cz) & (qf == cq))
+                def _():
+                    for n, tz, tq, slot in targets:
+                        a_copy(src, n, tz, tq, slot).start()
+
+    a_pass(0, a_ref)
+
+    upper, odd = qf // 2, qf % 2
+    away = 1 - zf
+    slots = (
+        flip((1 - upper) * away + upper * qf),
+        flip((1 - upper) * 2 + upper * ((1 - odd) * 3 + odd * away)),
+        flip((1 - upper) * 3 + upper * ((1 - odd) * away + odd * 2)),
+    )
+
+    def a_arrive(step):
+        slot = slots[step]
+        pltpu.make_async_copy(abuf.at[slot], abuf.at[slot], a_recv.at[slot]).wait()
+        a_pass(step + 1, abuf.at[slot])
+
+    def p_wait(block, r):
+        ref = pbuf.at[part(block, r), :]
+        pltpu.make_async_copy(ref, ref, p_recv.at[block * GRID + r]).wait()
+
+    layer_copies = []
+
+    def p_share(src, r, d):
+        for n, qt in ((0, across), (1, core_mate)):
+            cp = copy_to(src, pbuf.at[part(q, r), :], f_send.at[2 * d + n], p_recv.at[q * GRID + r], dev(z, qt))
+            cp.start()
+            layer_copies.append(cp)
+
+    p_share(p_ref.at[:, cols(z)], z, 0)
+    pbuf[part(q, z), :] = p_ref[:, cols(z)]
+    for d in (1, 3, 2):
+        r = (z + d) % GRID
+        p_wait(q, r)
+        p_share(pbuf.at[part(q, r), :], r, d)
+    a_arrive(0)
+    for d in (0, 1, 3, 2):
+        r = (z + d) % GRID
+        p_wait(across, r)
+        ref = pbuf.at[part(across, r), :]
+        cp = copy_to(ref, ref, g_send.at[d], p_recv.at[across * GRID + r], dev(z, core_mate))
+        cp.start()
+        layer_copies.append(cp)
+    for block in (core_mate, core_mate + 2 - 4 * y):
+        for r in range(GRID):
+            p_wait(block, r)
+
+    def lhat(block):
+        rows = pl.ds(pl.multiple_of(block * width, width), width)
+        return pbuf[rows, :] * pattern_ref[block, z].astype(jnp.float32)
+
+    def dot_t(left, right):
+        return lax.dot_general(left, right, (((0,), (0,)), ((), ())), precision=HIGHEST,
+                               preferred_element_type=jnp.float32)
+
+    acc[...] = dot_t(a_ref[...], lhat(z))
+    for step in range(3):
+        if step:
+            a_arrive(step)
+        slot = slots[step]
+        slot_f = flip(slot)
+        turned = (qf != zf) & (qf >= 2) & (slot_f < qf)
+
+        @pl.when(turned)
+        def _():
+            acc[...] += dot_t(abuf[slot], lhat(slot))
+
+        @pl.when(jnp.logical_not(turned))
+        def _():
+            acc[...] += jnp.dot(abuf[slot], lhat(slot), precision=HIGHEST, preferred_element_type=jnp.float32)
+
+    product = acc[...]
+    stage[...] = -(product * pattern_ref[q, z].astype(jnp.float32))
+    out_copies = []
+    for d in (1, 3, 2):
+        zt = (z + d) % GRID
+        cp = copy_to(stage.at[part(0, zt), :], off_ref.at[:, cols(z)], o_send.at[d], o_recv.at[z], dev(zt, q))
+        cp.start()
+        out_copies.append(cp)
+    dpart[...] = dot_t(lhat(q), product)
+    for d in (2, 1, 3):
+        qt = (q + d) % GRID
+        cp = copy_to(dpart.at[part(0, qt), :], dbuf.at[d - 1], d_send.at[d], d_recv.at[d - 1], dev(z, qt))
+        cp.start()
+        out_copies.append(cp)
+    off_ref[:, cols(z)] = stage[part(0, z), :]
+    total = dpart[part(0, q), :]
+    for d in (1, 2, 3):
+        pltpu.make_async_copy(dbuf.at[d - 1], dbuf.at[d - 1], d_recv.at[d - 1]).wait()
+        total = total + dbuf[d - 1]
+    for qt in range(GRID):
+        yt, ct = qt // 2, qt % 2
+        ebuf[qt] = total[yt * half_u:(yt + 1) * half_u, ct * half_v:(ct + 1) * half_v]
+    e_copies = [copy_to(ebuf.at[qt], dfin.at[z], e_send.at[qt], e_recv.at[z], dev(q, qt)) for qt in range(GRID)]
+    for qt in range(GRID):
+        own = (q == z) & (q == qt)
+
+        @pl.when(jnp.logical_not(own))
+        def _():
+            e_copies[qt].start()
+
+        @pl.when(own)
+        def _():
+            dfin[z] = ebuf[qt]
+
+    for d in (1, 3, 2):
+        zs = (z + d) % GRID
+        ref = off_ref.at[:, cols(zs)]
+        pltpu.make_async_copy(ref, ref, o_recv.at[zs]).wait()
+    for k in range(GRID):
+        @pl.when(jnp.logical_not((q == z) & (z == k)))
+        def _():
+            pltpu.make_async_copy(dfin.at[k], dfin.at[k], e_recv.at[k]).wait()
+        diag_ref[k] = dinv_ref[k] + dfin[k]
+
+    for cp in z_copies + layer_copies + out_copies:
+        cp.wait_send()
+    for qt in range(GRID):
+        @pl.when(jnp.logical_not((q == z) & (q == qt)))
+        def _():
+            e_copies[qt].wait_send()
+    for (cz, cq), routes in ROUTES.items():
+        @pl.when((zf == cz) & (qf == cq))
+        def _():
+            for targets in numbered(routes):
+                for n, tz, tq, slot in targets:
+                    a_copy(a_ref, n, tz, tq, slot).wait_send()
+
+
+def square_grid(inverse, panel, pattern, dinv):
+    width = inverse.shape[3]
+    sub, ncols = panel.shape[2], panel.shape[3]
+    vmem = pl.BlockSpec(memory_space=pltpu.VMEM)
+    dma = pltpu.SemaphoreType.DMA
+    f32 = jnp.float32
+    off, diagonal = pl.pallas_call(
+        kernel,
+        out_shape=(jax.ShapeDtypeStruct((sub, ncols), f32), jax.ShapeDtypeStruct(dinv.shape, f32)),
+        in_specs=[pl.BlockSpec(memory_space=pltpu.SMEM), vmem, vmem, vmem],
+        out_specs=(vmem, vmem),
+        scratch_shapes=[
+            pltpu.VMEM((GRID, width, width), f32),
+            pltpu.VMEM((GRID * width, width), f32),
+            pltpu.VMEM((width, width), f32),
+            pltpu.VMEM((width, width), f32),
+            pltpu.VMEM((width, width), f32),
+            pltpu.VMEM((GRID - 1, sub, width), f32),
+            pltpu.VMEM((GRID,) + dinv.shape[1:], f32),
+            pltpu.VMEM(dinv.shape, f32),
+            dma((8,)), dma((GRID,)), dma((GRID,)), dma((GRID * GRID,)), dma((2 * GRID,)), dma((GRID,)),
+            dma((GRID,)), dma((GRID,)), dma((GRID,)), dma((GRID,)), dma((GRID,)), dma((GRID,)),
+        ],
+        compiler_params=pltpu.CompilerParams(
+            collective_id=0, has_side_effects=True, vmem_limit_bytes=32 * 1024 * 1024),
+    )(pattern, inverse.reshape(inverse.shape[2:]), panel.reshape(panel.shape[2:]), dinv)
+    return off.reshape(panel.shape), diagonal
+
+
+def fits_square_grid(mesh_shape, inverse, panel, pattern, dinv):
+    n_row, n_col = mesh_shape["row"], mesh_shape["col"]
+    width = inverse.shape[3]
+    return (
+        n_row == 2 * GRID and n_col == 2
+        and inverse.shape[2] == width and width % 128 == 0
+        and pattern.shape == (GRID, GRID)
+        and panel.shape[2] * GRID == width and panel.shape[3] == GRID * width
+        and dinv.shape == (GRID, width // n_row, width // n_col)
+    )
+
+
+def body(inverse, panel, pattern, dinv):
+    sizes = {"row": lax.axis_size("row"), "col": lax.axis_size("col")}
+    if fits_square_grid(sizes, inverse, panel, pattern, dinv):
+        return square_grid(inverse, panel, pattern, dinv)
+    return general_body(inverse, panel, pattern, dinv)
+
+
 def solution(mesh):
     return jax.shard_map(
         body,

time: 162 us -> 49 us (0.30)
  waiting for transfers between devices: 126 us -> 0 us
  Pallas kernels: 0 us -> 43.4 us
  starting transfers between devices: 13.8 us -> 0 us
  between operations: 14.2 us -> 0.65 us
  matrix products: 2.47 us -> 0 us
  other arithmetic: 2.45 us -> 0 us
    ppermute x8 -> x0, waiting for transfers between devices: 67.2 us -> none  [swapped(): return lax.ppermute(value, axis, pairs)]
    reduce_scatter x1 -> x0, waiting for transfers between devices: 58.4 us -> none  [body(): lax.psum_scatter(arranged, ('row', 'col'), scatter_dimension=0, tiled=True)]
    pallas_call x0 -> x1, Pallas kernels: none -> 43.4 us  [square_grid(): pl.pallas_call(kernel, out_shape=(jax.ShapeDtypeStruct((sub, ncols), f32)...]
    ppermute x8 -> x0, starting transfers between devices: 13.7 us -> none  [swapped(): return lax.ppermute(value, axis, pairs)]
    unnamed x10, local copies, waits for them, and re-layouts: 1.71 us -> 4.75 us
    dot_general x3 -> x0, matrix products: 2.47 us -> none  [the longest x1 1.15 us: body(): jnp.einsum('rkw,rkv->kwv', lhat_piece.reshape(rows_dev, sup_count, sup_wi...]
  transfers between devices with their start and end apart: 9 -> 0, of which waited for: 9 -> 0; matrix products, arithmetic and copies ran while one was open for 0% -> 0% of each run, Pallas kernels for 0% -> 0%
where the time goes in v1:
time: 49 us; the launch traced here: 48.8 us
  Pallas kernels  43.4 us (89%)
  local copies, waits for them, and re-layouts  4.75 us (10%)
  between operations  0.65 us (1%)
    pallas_call x1, Pallas kernels, square_grid(): pl.pallas_call(kernel, out_shape=(jax.ShapeDtypeStruct((sub, ncols), f32)...  43.4 us
    unnamed x10, local copies, waits for them, and re-layouts  4.75 us

profile of v1, /device:TPU:0, one launch (start us, length us, event | category | flops | bytes accessed | tf_op | source)
XLA Modules:
  0.0 48.8 jit_solution(6687175557531597068)
XLA Ops:
  0.6 0.0 copy-start.3
  0.6 0.7 %copy-done.3 = s32[4,4]{1,0:T(4,128)S(1)} copy-done((s32[4,4]{1,0:T(4,128)S(1)}, s32[4,4]{1,0:T(4,128)}, u32[]{:S(2)}) %copy-start.3) | copy-done | bytes 88
  1.3 0.0 copy-start
  1.3 0.9 %copy-done = f32[1,1,256,256]{3,2,1,0:T(8,128)S(1)} copy-done((f32[1,1,256,256]{3,2,1,0:T(8,128)S(1)}, f32[1,1,256,256]{3,2,1,0:T(8,128)}, u32[]{:S(2)}) %copy-start) | copy-done | bytes 262168
  2.3 0.0 copy-start.1
  2.3 0.9 %copy-done.1 = f32[1,1,64,1024]{3,2,1,0:T(8,128)S(1)} copy-done((f32[1,1,64,1024]{3,2,1,0:T(8,128)S(1)}, f32[1,1,64,1024]{3,2,1,0:T(8,128)}, u32[]{:S(2)}) %copy-start.1) | copy-done | bytes 262168
  3.2 0.0 copy-start.2
  3.2 0.8 %copy-done.2 = f32[4,32,128]{2,1,0:T(8,128)S(1)} copy-done((f32[4,32,128]{2,1,0:T(8,128)S(1)}, f32[4,32,128]{2,1,0:T(8,128)}, u32[]{:S(2)}) %copy-start.2) | copy-done | bytes 65560
  4.1 43.4 %shard_map.59 = (f32[64,1024]{1,0:T(8,128)S(1)}, f32[4,32,128]{2,1,0:T(8,128)S(1)}) custom-call(s32[4,4]{1,0:T(4,128)S(1)} %copy-done.3, f32[256,256]{1,0:T(8,128)S(1)} %bitcast.3, f32[64,1024]{1,0:T(8,128)S(1)} %bitcast.4, f32[4,32,128]{2,1,0:T(8,128)S(1)} %copy-done.2), custom_call_target="tpu_custom_call" | custom-call | tf_op jit(solution)/shard_map/pallas_call | solution.py:338
  47.4 0.7 %copy.8 = f32[1,1,64,1024]{3,2,1,0:T(8,128)} copy(f32[1,1,64,1024]{3,2,1,0:T(8,128)S(1)} %bitcast.5) | data formatting | bytes 524288
  48.1 0.6 %copy.9 = f32[4,32,128]{2,1,0:T(8,128)} copy(f32[4,32,128]{2,1,0:T(8,128)S(1)} %get-tuple-element.9) | data formatting | bytes 131072
Async XLA Ops:
  0.6 0.7 %copy-start.3 = (s32[4,4]{1,0:T(4,128)S(1)}, s32[4,4]{1,0:T(4,128)}, u32[]{:S(2)}) copy-start(s32[4,4]{1,0:T(4,128)} %pattern_ref.1) | copy-start | bytes 196
  1.3 0.9 %copy-start = (f32[1,1,256,256]{3,2,1,0:T(8,128)S(1)}, f32[1,1,256,256]{3,2,1,0:T(8,128)}, u32[]{:S(2)}) copy-start(f32[1,1,256,256]{3,2,1,0:T(8,128)} %param.4) | copy-start | bytes 786436
  2.3 0.9 %copy-start.1 = (f32[1,1,64,1024]{3,2,1,0:T(8,128)S(1)}, f32[1,1,64,1024]{3,2,1,0:T(8,128)}, u32[]{:S(2)}) copy-start(f32[1,1,64,1024]{3,2,1,0:T(8,128)} %param.5) | copy-start | bytes 786436
  3.2 0.8 %copy-start.2 = (f32[4,32,128]{2,1,0:T(8,128)S(1)}, f32[4,32,128]{2,1,0:T(8,128)}, u32[]{:S(2)}) copy-start(f32[4,32,128]{2,1,0:T(8,128)} %dinv_ref.1) | copy-start | bytes 196612

commit v2 on v1

--- a/solution.py
+++ b/solution.py
@@ -117,6 +117,7 @@
 MESH = pl.DeviceIdType.MESH
 HIGHEST = lax.Precision.HIGHEST
 GRID = 4
+CHUNKS = 4
 
 ROUTES = {
     (0, 0): ([(1, 0, 0)], [], [(1, 0, 2)], [(1, 0, 3)]),
@@ -139,12 +140,13 @@
     return out
 
 
-def kernel(pattern_ref, a_ref, p_ref, dinv_ref, off_ref, diag_ref,
-           abuf, pbuf, acc, stage, dpart, dbuf, ebuf, dfin,
+def kernel(pattern_hbm, a_hbm, p_hbm, dinv_hbm, off_ref, diag_ref,
+           pattern_ref, a_ref, dinv_ref, l_sem, abuf, pbuf, acc, stage, dpart, dbuf, ebuf, dfin,
            a_send, a_recv, p_send, p_recv, f_send, g_send, o_send, o_recv,
            d_send, d_recv, e_send, e_recv):
-    width = a_ref.shape[0]
-    sub = p_ref.shape[0]
+    width = a_hbm.shape[0]
+    sub = p_hbm.shape[0]
+    slab = width // CHUNKS
     half_u, half_v = dinv_ref.shape[1], dinv_ref.shape[2]
     pole = lax.axis_index("pole")
     row = lax.axis_index("row")
@@ -167,6 +169,21 @@
             src_ref=src, dst_ref=dst, send_sem=send, recv_sem=recv,
             device_id=where, device_id_type=MESH)
 
+    def cols(k):
+        return pl.ds(pl.multiple_of(k * width, width), width)
+
+    def part(block, r):
+        return pl.ds(pl.multiple_of(block * width + r * sub, sub), sub)
+
+    loads = [
+        pltpu.make_async_copy(pattern_hbm, pattern_ref, l_sem.at[0]),
+        pltpu.make_async_copy(p_hbm.at[:, cols(z)], pbuf.at[part(q, z), :], l_sem.at[1]),
+        pltpu.make_async_copy(a_hbm, a_ref, l_sem.at[2]),
+        pltpu.make_async_copy(dinv_hbm, dinv_ref, l_sem.at[3]),
+    ]
+    for cp in loads:
+        cp.start()
+
     barrier = pltpu.get_barrier_semaphore()
     me = z * GRID + q
     for d in range(1, GRID * GRID):
@@ -177,32 +194,29 @@
     core_mate = q + 1 - 2 * c
     across = q + 2 - 4 * y
 
-    def cols(k):
-        return pl.ds(pl.multiple_of(k * width, width), width)
-
-    def part(block, r):
-        return pl.ds(pl.multiple_of(block * width + r * sub, sub), sub)
-
     z_copies = []
     for d in (1, 3, 2):
         zt = (z + d) % GRID
-        cp = copy_to(p_ref.at[:, cols(zt)], pbuf.at[part(q, z), :], p_send.at[d], p_recv.at[q * GRID + z], dev(zt, q))
+        cp = copy_to(p_hbm.at[:, cols(zt)], pbuf.at[part(q, z), :], p_send.at[d], p_recv.at[q * GRID + z], dev(zt, q))
         cp.start()
         z_copies.append(cp)
 
-    def a_copy(src, n, tz, tq, slot):
-        return copy_to(src, abuf.at[flip(slot)], a_send.at[n], a_recv.at[flip(slot)], dev(flip(tz), flip(tq)))
-
-    def a_pass(step, src):
+    def a_copy(src, n, tz, tq, slot, chunk):
+        rows = pl.ds(chunk * slab, slab)
+        return copy_to(src.at[rows, :], abuf.at[flip(slot), rows, :], a_send.at[n * CHUNKS + chunk],
+                       a_recv.at[flip(slot) * CHUNKS + chunk], dev(flip(tz), flip(tq)))
+
+    def a_pass(step, src, chunk):
         for (cz, cq), routes in ROUTES.items():
             targets = numbered(routes)[step]
             if targets:
                 @pl.when((zf == cz) & (qf == cq))
                 def _():
                     for n, tz, tq, slot in targets:
-                        a_copy(src, n, tz, tq, slot).start()
-
-    a_pass(0, a_ref)
+                        a_copy(src, n, tz, tq, slot, chunk).start()
+
+    for chunk in range(CHUNKS):
+        a_pass(0, a_hbm, chunk)
 
     upper, odd = qf // 2, qf % 2
     away = 1 - zf
@@ -214,8 +228,10 @@
 
     def a_arrive(step):
         slot = slots[step]
-        pltpu.make_async_copy(abuf.at[slot], abuf.at[slot], a_recv.at[slot]).wait()
-        a_pass(step + 1, abuf.at[slot])
+        for chunk in range(CHUNKS):
+            ref = abuf.at[slot, pl.ds(chunk * slab, slab), :]
+            pltpu.make_async_copy(ref, ref, a_recv.at[slot * CHUNKS + chunk]).wait()
+            a_pass(step + 1, abuf.at[slot], chunk)
 
     def p_wait(block, r):
         ref = pbuf.at[part(block, r), :]
@@ -229,8 +245,9 @@
             cp.start()
             layer_copies.append(cp)
 
-    p_share(p_ref.at[:, cols(z)], z, 0)
-    pbuf[part(q, z), :] = p_ref[:, cols(z)]
+    p_share(p_hbm.at[:, cols(z)], z, 0)
+    for cp in loads:
+        cp.wait()
     for d in (1, 3, 2):
         r = (z + d) % GRID
         p_wait(q, r)
@@ -326,7 +343,8 @@
         def _():
             for targets in numbered(routes):
                 for n, tz, tq, slot in targets:
-                    a_copy(a_ref, n, tz, tq, slot).wait_send()
+                    for chunk in range(CHUNKS):
+                        a_copy(a_ref, n, tz, tq, slot, chunk).wait_send()
 
 
 def square_grid(inverse, panel, pattern, dinv):
@@ -338,9 +356,13 @@
     off, diagonal = pl.pallas_call(
         kernel,
         out_shape=(jax.ShapeDtypeStruct((sub, ncols), f32), jax.ShapeDtypeStruct(dinv.shape, f32)),
-        in_specs=[pl.BlockSpec(memory_space=pltpu.SMEM), vmem, vmem, vmem],
+        in_specs=[pl.BlockSpec(memory_space=pl.ANY)] * 4,
         out_specs=(vmem, vmem),
         scratch_shapes=[
+            pltpu.SMEM(pattern.shape, pattern.dtype),
+            pltpu.VMEM((width, width), f32),
+            pltpu.VMEM(dinv.shape, f32),
+            dma((4,)),
             pltpu.VMEM((GRID, width, width), f32),
             pltpu.VMEM((GRID * width, width), f32),
             pltpu.VMEM((width, width), f32),
@@ -349,11 +371,11 @@
             pltpu.VMEM((GRID - 1, sub, width), f32),
             pltpu.VMEM((GRID,) + dinv.shape[1:], f32),
             pltpu.VMEM(dinv.shape, f32),
-            dma((8,)), dma((GRID,)), dma((GRID,)), dma((GRID * GRID,)), dma((2 * GRID,)), dma((GRID,)),
+            dma((8 * CHUNKS,)), dma((GRID * CHUNKS,)), dma((GRID,)), dma((GRID * GRID,)), dma((2 * GRID,)), dma((GRID,)),
             dma((GRID,)), dma((GRID,)), dma((GRID,)), dma((GRID,)), dma((GRID,)), dma((GRID,)),
         ],
         compiler_params=pltpu.CompilerParams(
-            collective_id=0, has_side_effects=True, vmem_limit_bytes=32 * 1024 * 1024),
+            collective_id=0, has_side_effects=True, vmem_limit_bytes=56 * 1024 * 1024),
     )(pattern, inverse.reshape(inverse.shape[2:]), panel.reshape(panel.shape[2:]), dinv)
     return off.reshape(panel.shape), diagonal
 

time: 49 us -> 45.3 us (0.924)
  local copies, waits for them, and re-layouts: 4.75 us -> 2.34 us
  Pallas kernels: 43.4 us -> 42.2 us
    unnamed x10 -> x4, local copies, waits for them, and re-layouts: 4.75 us -> 2.34 us
    pallas_call x1, Pallas kernels: 43.4 us -> 42.2 us  [square_grid(): pl.pallas_call(kernel, out_shape=(jax.ShapeDtypeStruct((sub, ncols), f32)...]
where the time goes in v2:
time: 45.3 us; the launch traced here: 45.2 us
  Pallas kernels  42.2 us (93%)
  local copies, waits for them, and re-layouts  2.34 us (5%)
  between operations  0.65 us (1%)
    pallas_call x1, Pallas kernels, square_grid(): pl.pallas_call(kernel, out_shape=(jax.ShapeDtypeStruct((sub, ncols), f32)...  42.2 us
    unnamed x4, local copies, waits for them, and re-layouts  2.34 us

profile of v2, /device:TPU:0, one launch (start us, length us, event | category | flops | bytes accessed | tf_op | source)
XLA Modules:
  0.0 45.2 jit_solution(110624060550071870)
XLA Ops:
  0.6 42.2 %shard_map.59 = (f32[64,1024]{1,0:T(8,128)}, f32[4,32,128]{2,1,0:T(8,128)}) custom-call(s32[4,4]{1,0:T(4,128)} %pattern_hbm.1, f32[256,256]{1,0:T(8,128)} %bitcast.3, f32[64,1024]{1,0:T(8,128)} %bitcast.4, f32[4,32,128]{2,1,0:T(8,128)} %dinv_hbm.1), custom_call_target="tpu_custom_call" | custom-call | tf_op jit(solution)/shard_map/pallas_call | solution.py:356
  42.8 0.0 copy-start
  42.8 1.7 %copy.8 = f32[1,1,64,1024]{3,2,1,0:T(8,128)} copy(f32[1,1,64,1024]{3,2,1,0:T(8,128)} %bitcast.5) | data formatting | bytes 524288
  44.5 0.0 copy-done
  44.5 0.6 %copy.9 = f32[4,32,128]{2,1,0:T(8,128)} copy(f32[4,32,128]{2,1,0:T(8,128)S(1)} %copy-done) | data formatting | bytes 131072
Async XLA Ops:
  42.8 1.7 %copy-start = (f32[4,32,128]{2,1,0:T(8,128)S(1)}, f32[4,32,128]{2,1,0:T(8,128)}, u32[]{:S(2)}) copy-start(f32[4,32,128]{2,1,0:T(8,128)} %get-tuple-element.9) | copy-start | bytes 196612

commit v3 on v2

--- a/solution.py
+++ b/solution.py
@@ -130,6 +130,15 @@
     (1, 3): ([(1, 1, 3)], [(0, 3, 3)], [], []),
 }
 
+RELAY_AT = (
+    {(1, 0): (0,), (1, 1): (0,), (1, 2): (0,)},
+    {(0, 0): (1,), (1, 1): (1,)},
+    {(0, 0): (2,), (1, 1): (2,), (1, 2): (1,), (1, 3): (0,)},
+    {(0, 2): (1,)},
+    {(1, 0): (1,), (0, 1): (1,)},
+    {(1, 0): (2,), (0, 1): (2,)},
+)
+
 
 def numbered(routes):
     count = 0
@@ -185,14 +194,25 @@
         cp.start()
 
     barrier = pltpu.get_barrier_semaphore()
-    me = z * GRID + q
-    for d in range(1, GRID * GRID):
-        other = (me + d) % (GRID * GRID)
-        pl.semaphore_signal(barrier, inc=1, device_id=dev(other // GRID, other % GRID), device_id_type=MESH)
-    pl.semaphore_wait(barrier, GRID * GRID - 1)
+    for d in range(1, GRID):
+        pl.semaphore_signal(barrier, inc=1, device_id=dev(z, (q + d) % GRID), device_id_type=MESH)
+        pl.semaphore_signal(barrier, inc=1, device_id=dev((z + d) % GRID, q), device_id_type=MESH)
+    pl.semaphore_wait(barrier, 2 * (GRID - 1))
 
     core_mate = q + 1 - 2 * c
     across = q + 2 - 4 * y
+
+    def a_copy(src, n, tz, tq, slot, chunk):
+        rows = pl.ds(chunk * slab, slab)
+        return copy_to(src.at[rows, :], abuf.at[flip(slot), rows, :], a_send.at[n * CHUNKS + chunk],
+                       a_recv.at[flip(slot) * CHUNKS + chunk], dev(flip(tz), flip(tq)))
+
+    for (cz, cq), routes in ROUTES.items():
+        @pl.when((zf == cz) & (qf == cq))
+        def _():
+            for chunk in range(CHUNKS):
+                for n, tz, tq, slot in numbered(routes)[0]:
+                    a_copy(a_hbm, n, tz, tq, slot, chunk).start()
 
     z_copies = []
     for d in (1, 3, 2):
@@ -200,23 +220,6 @@
         cp = copy_to(p_hbm.at[:, cols(zt)], pbuf.at[part(q, z), :], p_send.at[d], p_recv.at[q * GRID + z], dev(zt, q))
         cp.start()
         z_copies.append(cp)
-
-    def a_copy(src, n, tz, tq, slot, chunk):
-        rows = pl.ds(chunk * slab, slab)
-        return copy_to(src.at[rows, :], abuf.at[flip(slot), rows, :], a_send.at[n * CHUNKS + chunk],
-                       a_recv.at[flip(slot) * CHUNKS + chunk], dev(flip(tz), flip(tq)))
-
-    def a_pass(step, src, chunk):
-        for (cz, cq), routes in ROUTES.items():
-            targets = numbered(routes)[step]
-            if targets:
-                @pl.when((zf == cz) & (qf == cq))
-                def _():
-                    for n, tz, tq, slot in targets:
-                        a_copy(src, n, tz, tq, slot, chunk).start()
-
-    for chunk in range(CHUNKS):
-        a_pass(0, a_hbm, chunk)
 
     upper, odd = qf // 2, qf % 2
     away = 1 - zf
@@ -226,12 +229,30 @@
         flip((1 - upper) * 3 + upper * ((1 - odd) * away + odd * 2)),
     )
 
+    def a_wait(step, chunk):
+        slot = slots[step]
+        ref = abuf.at[slot, pl.ds(chunk * slab, slab), :]
+        pltpu.make_async_copy(ref, ref, a_recv.at[slot * CHUNKS + chunk]).wait()
+
+    def a_relay(place):
+        for (cz, cq), routes in ROUTES.items():
+            steps = RELAY_AT[place].get((cz, cq), ())
+            if steps:
+                @pl.when((zf == cz) & (qf == cq))
+                def _():
+                    for step in steps:
+                        for chunk in range(CHUNKS):
+                            a_wait(step, chunk)
+                            for n, tz, tq, slot in numbered(routes)[step + 1]:
+                                a_copy(abuf.at[slots[step]], n, tz, tq, slot, chunk).start()
+
     def a_arrive(step):
-        slot = slots[step]
-        for chunk in range(CHUNKS):
-            ref = abuf.at[slot, pl.ds(chunk * slab, slab), :]
-            pltpu.make_async_copy(ref, ref, a_recv.at[slot * CHUNKS + chunk]).wait()
-            a_pass(step + 1, abuf.at[slot], chunk)
+        for (cz, cq), routes in ROUTES.items():
+            if not routes[step + 1]:
+                @pl.when((zf == cz) & (qf == cq))
+                def _():
+                    for chunk in range(CHUNKS):
+                        a_wait(step, chunk)
 
     def p_wait(block, r):
         ref = pbuf.at[part(block, r), :]
@@ -248,11 +269,13 @@
     p_share(p_hbm.at[:, cols(z)], z, 0)
     for cp in loads:
         cp.wait()
-    for d in (1, 3, 2):
+    a_relay(0)
+    for place, d in enumerate((1, 3, 2)):
         r = (z + d) % GRID
         p_wait(q, r)
         p_share(pbuf.at[part(q, r), :], r, d)
-    a_arrive(0)
+        a_relay(place + 1)
+    a_relay(4)
     for d in (0, 1, 3, 2):
         r = (z + d) % GRID
         p_wait(across, r)
@@ -260,6 +283,7 @@
         cp = copy_to(ref, ref, g_send.at[d], p_recv.at[across * GRID + r], dev(z, core_mate))
         cp.start()
         layer_copies.append(cp)
+    a_relay(5)
     for block in (core_mate, core_mate + 2 - 4 * y):
         for r in range(GRID):
             p_wait(block, r)
@@ -274,8 +298,7 @@
 
     acc[...] = dot_t(a_ref[...], lhat(z))
     for step in range(3):
-        if step:
-            a_arrive(step)
+        a_arrive(step)
         slot = slots[step]
         slot_f = flip(slot)
         turned = (qf != zf) & (qf >= 2) & (slot_f < qf)
@@ -296,48 +319,38 @@
         cp = copy_to(stage.at[part(0, zt), :], off_ref.at[:, cols(z)], o_send.at[d], o_recv.at[z], dev(zt, q))
         cp.start()
         out_copies.append(cp)
-    dpart[...] = dot_t(lhat(q), product)
+    terms = dot_t(lhat(q), product)
+    for zt in range(GRID):
+        for qt in range(GRID):
+            u, v = zt * sub + (qt // 2) * half_u, (qt % 2) * half_v
+            dpart[qt, zt] = terms[u:u + half_u, v:v + half_v]
     for d in (2, 1, 3):
         qt = (q + d) % GRID
-        cp = copy_to(dpart.at[part(0, qt), :], dbuf.at[d - 1], d_send.at[d], d_recv.at[d - 1], dev(z, qt))
+        cp = copy_to(dpart.at[qt], dbuf.at[d - 1], d_send.at[d], d_recv.at[d - 1], dev(z, qt))
         cp.start()
         out_copies.append(cp)
     off_ref[:, cols(z)] = stage[part(0, z), :]
-    total = dpart[part(0, q), :]
+    total = dpart[q]
     for d in (1, 2, 3):
         pltpu.make_async_copy(dbuf.at[d - 1], dbuf.at[d - 1], d_recv.at[d - 1]).wait()
         total = total + dbuf[d - 1]
-    for qt in range(GRID):
-        yt, ct = qt // 2, qt % 2
-        ebuf[qt] = total[yt * half_u:(yt + 1) * half_u, ct * half_v:(ct + 1) * half_v]
-    e_copies = [copy_to(ebuf.at[qt], dfin.at[z], e_send.at[qt], e_recv.at[z], dev(q, qt)) for qt in range(GRID)]
-    for qt in range(GRID):
-        own = (q == z) & (q == qt)
-
-        @pl.when(jnp.logical_not(own))
-        def _():
-            e_copies[qt].start()
-
-        @pl.when(own)
-        def _():
-            dfin[z] = ebuf[qt]
-
+    ebuf[...] = total
+    for d in (1, 3, 2):
+        zt = (z + d) % GRID
+        cp = copy_to(ebuf.at[zt], dfin.at[z], e_send.at[d], e_recv.at[z], dev(zt, q))
+        cp.start()
+        out_copies.append(cp)
+    diag_ref[z] = dinv_ref[z] + ebuf[z]
+    for d in (1, 3, 2):
+        k = (z + d) % GRID
+        pltpu.make_async_copy(dfin.at[k], dfin.at[k], e_recv.at[k]).wait()
+        diag_ref[k] = dinv_ref[k] + dfin[k]
     for d in (1, 3, 2):
         zs = (z + d) % GRID
         ref = off_ref.at[:, cols(zs)]
         pltpu.make_async_copy(ref, ref, o_recv.at[zs]).wait()
-    for k in range(GRID):
-        @pl.when(jnp.logical_not((q == z) & (z == k)))
-        def _():
-            pltpu.make_async_copy(dfin.at[k], dfin.at[k], e_recv.at[k]).wait()
-        diag_ref[k] = dinv_ref[k] + dfin[k]
-
     for cp in z_copies + layer_copies + out_copies:
         cp.wait_send()
-    for qt in range(GRID):
-        @pl.when(jnp.logical_not((q == z) & (q == qt)))
-        def _():
-            e_copies[qt].wait_send()
     for (cz, cq), routes in ROUTES.items():
         @pl.when((zf == cz) & (qf == cq))
         def _():
@@ -356,7 +369,7 @@
     off, diagonal = pl.pallas_call(
         kernel,
         out_shape=(jax.ShapeDtypeStruct((sub, ncols), f32), jax.ShapeDtypeStruct(dinv.shape, f32)),
-        in_specs=[pl.BlockSpec(memory_space=pl.ANY)] * 4,
+        in_specs=[pl.BlockSpec(memory_space=pltpu.HBM)] * 4,
         out_specs=(vmem, vmem),
         scratch_shapes=[
             pltpu.SMEM(pattern.shape, pattern.dtype),
@@ -367,9 +380,9 @@
             pltpu.VMEM((GRID * width, width), f32),
             pltpu.VMEM((width, width), f32),
             pltpu.VMEM((width, width), f32),
-            pltpu.VMEM((width, width), f32),
-            pltpu.VMEM((GRID - 1, sub, width), f32),
-            pltpu.VMEM((GRID,) + dinv.shape[1:], f32),
+            pltpu.VMEM((GRID,) + dinv.shape, f32),
+            pltpu.VMEM((GRID - 1,) + dinv.shape, f32),
+            pltpu.VMEM(dinv.shape, f32),
             pltpu.VMEM(dinv.shape, f32),
             dma((8 * CHUNKS,)), dma((GRID * CHUNKS,)), dma((GRID,)), dma((GRID * GRID,)), dma((2 * GRID,)), dma((GRID,)),
             dma((GRID,)), dma((GRID,)), dma((GRID,)), dma((GRID,)), dma((GRID,)), dma((GRID,)),

time: 45.3 us -> 41.6 us (0.918)
  Pallas kernels: 42.2 us -> 38.4 us
    pallas_call x1, Pallas kernels: 42.2 us -> 38.4 us  [square_grid(): pl.pallas_call(kernel, out_shape=(jax.ShapeDtypeStruct((sub, ncols), f32)...]
where the time goes in v3:
time: 41.6 us; the launch traced here: 41.4 us
  Pallas kernels  38.4 us (92%)
  local copies, waits for them, and re-layouts  2.34 us (6%)
  between operations  0.65 us (2%)
    pallas_call x1, Pallas kernels, square_grid(): pl.pallas_call(kernel, out_shape=(jax.ShapeDtypeStruct((sub, ncols), f32)...  38.4 us
    unnamed x4, local copies, waits for them, and re-layouts  2.34 us

profile of v3, /device:TPU:0, one launch (start us, length us, event | category | flops | bytes accessed | tf_op | source)
XLA Modules:
  0.0 41.4 jit_solution(13320041708250805979)
XLA Ops:
  0.6 38.4 %shard_map.59 = (f32[64,1024]{1,0:T(8,128)}, f32[4,32,128]{2,1,0:T(8,128)}) custom-call(s32[4,4]{1,0:T(4,128)} %pattern_hbm.1, f32[256,256]{1,0:T(8,128)} %bitcast.3, f32[64,1024]{1,0:T(8,128)} %bitcast.4, f32[4,32,128]{2,1,0:T(8,128)} %dinv_hbm.1), custom_call_target="tpu_custom_call" | custom-call | tf_op jit(solution)/shard_map/pallas_call | solution.py:369
  39.1 0.0 copy-start
  39.1 1.7 %copy.8 = f32[1,1,64,1024]{3,2,1,0:T(8,128)} copy(f32[1,1,64,1024]{3,2,1,0:T(8,128)} %bitcast.5) | data formatting | bytes 524288
  40.8 0.0 copy-done
  40.8 0.6 %copy.9 = f32[4,32,128]{2,1,0:T(8,128)} copy(f32[4,32,128]{2,1,0:T(8,128)S(1)} %copy-done) | data formatting | bytes 131072
Async XLA Ops:
  39.1 1.7 %copy-start = (f32[4,32,128]{2,1,0:T(8,128)S(1)}, f32[4,32,128]{2,1,0:T(8,128)}, u32[]{:S(2)}) copy-start(f32[4,32,128]{2,1,0:T(8,128)} %get-tuple-element.9) | copy-start | bytes 196612

commit v4 on v3

--- a/solution.py
+++ b/solution.py
@@ -118,6 +118,7 @@
 HIGHEST = lax.Precision.HIGHEST
 GRID = 4
 CHUNKS = 4
+PIECES = 2
 
 ROUTES = {
     (0, 0): ([(1, 0, 0)], [], [(1, 0, 2)], [(1, 0, 3)]),
@@ -130,13 +131,23 @@
     (1, 3): ([(1, 1, 3)], [(0, 3, 3)], [], []),
 }
 
+def one(step):
+    return [(step, chunk) for chunk in range(CHUNKS)]
+
+
+def both(chunks):
+    return [(step, chunk) for chunk in chunks for step in (1, 2)]
+
+
 RELAY_AT = (
-    {(1, 0): (0,), (1, 1): (0,), (1, 2): (0,)},
-    {(0, 0): (1,), (1, 1): (1,)},
-    {(0, 0): (2,), (1, 1): (2,), (1, 2): (1,), (1, 3): (0,)},
-    {(0, 2): (1,)},
-    {(1, 0): (1,), (0, 1): (1,)},
-    {(1, 0): (2,), (0, 1): (2,)},
+    {(1, 0): one(0), (1, 1): one(0) + both(range(CHUNKS)), (1, 2): one(0), (0, 0): both(range(CHUNKS))},
+    {},
+    {(1, 2): one(1), (1, 3): one(0)},
+    {(0, 2): one(1)},
+    {(1, 0): both((0,)), (0, 1): both((0,))},
+    {(1, 0): both((1,)), (0, 1): both((1,))},
+    {(1, 0): both((2,)), (0, 1): both((2,))},
+    {(1, 0): both((3,)), (0, 1): both((3,))},
 )
 
 
@@ -150,7 +161,7 @@
 
 
 def kernel(pattern_hbm, a_hbm, p_hbm, dinv_hbm, off_ref, diag_ref,
-           pattern_ref, a_ref, dinv_ref, l_sem, abuf, pbuf, acc, stage, dpart, dbuf, ebuf, dfin,
+           pattern_ref, a_ref, dinv_ref, l_sem, w_sem, abuf, pbuf, acc, stage, dpart, dbuf, ebuf, dfin,
            a_send, a_recv, p_send, p_recv, f_send, g_send, o_send, o_recv,
            d_send, d_recv, e_send, e_recv):
     width = a_hbm.shape[0]
@@ -240,11 +251,10 @@
             if steps:
                 @pl.when((zf == cz) & (qf == cq))
                 def _():
-                    for step in steps:
-                        for chunk in range(CHUNKS):
-                            a_wait(step, chunk)
-                            for n, tz, tq, slot in numbered(routes)[step + 1]:
-                                a_copy(abuf.at[slots[step]], n, tz, tq, slot, chunk).start()
+                    for step, chunk in steps:
+                        a_wait(step, chunk)
+                        for n, tz, tq, slot in numbered(routes)[step + 1]:
+                            a_copy(abuf.at[slots[step]], n, tz, tq, slot, chunk).start()
 
     def a_arrive(step):
         for (cz, cq), routes in ROUTES.items():
@@ -275,15 +285,14 @@
         p_wait(q, r)
         p_share(pbuf.at[part(q, r), :], r, d)
         a_relay(place + 1)
-    a_relay(4)
-    for d in (0, 1, 3, 2):
+    for place, d in enumerate((0, 1, 3, 2)):
+        a_relay(4 + place)
         r = (z + d) % GRID
         p_wait(across, r)
         ref = pbuf.at[part(across, r), :]
         cp = copy_to(ref, ref, g_send.at[d], p_recv.at[across * GRID + r], dev(z, core_mate))
         cp.start()
         layer_copies.append(cp)
-    a_relay(5)
     for block in (core_mate, core_mate + 2 - 4 * y):
         for r in range(GRID):
             p_wait(block, r)
@@ -329,7 +338,8 @@
         cp = copy_to(dpart.at[qt], dbuf.at[d - 1], d_send.at[d], d_recv.at[d - 1], dev(z, qt))
         cp.start()
         out_copies.append(cp)
-    off_ref[:, cols(z)] = stage[part(0, z), :]
+    writes = [pltpu.make_async_copy(stage.at[part(0, z), :], off_ref.at[:, cols(z)], w_sem.at[0])]
+    writes[0].start()
     total = dpart[q]
     for d in (1, 2, 3):
         pltpu.make_async_copy(dbuf.at[d - 1], dbuf.at[d - 1], d_recv.at[d - 1]).wait()
@@ -340,15 +350,19 @@
         cp = copy_to(ebuf.at[zt], dfin.at[z], e_send.at[d], e_recv.at[z], dev(zt, q))
         cp.start()
         out_copies.append(cp)
-    diag_ref[z] = dinv_ref[z] + ebuf[z]
+    dinv_ref[z] = dinv_ref[z] + ebuf[z]
     for d in (1, 3, 2):
         k = (z + d) % GRID
         pltpu.make_async_copy(dfin.at[k], dfin.at[k], e_recv.at[k]).wait()
-        diag_ref[k] = dinv_ref[k] + dfin[k]
+        dinv_ref[k] = dinv_ref[k] + dfin[k]
+    writes.append(pltpu.make_async_copy(dinv_ref, diag_ref, w_sem.at[1]))
+    writes[1].start()
     for d in (1, 3, 2):
         zs = (z + d) % GRID
         ref = off_ref.at[:, cols(zs)]
         pltpu.make_async_copy(ref, ref, o_recv.at[zs]).wait()
+    for cp in writes:
+        cp.wait()
     for cp in z_copies + layer_copies + out_copies:
         cp.wait_send()
     for (cz, cq), routes in ROUTES.items():
@@ -360,22 +374,44 @@
                         a_copy(a_ref, n, tz, tq, slot, chunk).wait_send()
 
 
+def hand_over(off_in, diag_in, off_out, diag_out, off_held, diag_held, off_sem, diag_sem):
+    rows = off_in.shape[0] // PIECES
+    pairs = [(
+        pltpu.make_async_copy(diag_in, diag_held, diag_sem.at[0]),
+        pltpu.make_async_copy(diag_held, diag_out, diag_sem.at[1]),
+    )]
+    for n in range(PIECES):
+        piece = pl.ds(n * rows, rows)
+        pairs.append((
+            pltpu.make_async_copy(off_in.at[piece, :], off_held.at[piece, :], off_sem.at[0, n]),
+            pltpu.make_async_copy(off_held.at[piece, :], off_out.at[piece, :], off_sem.at[1, n]),
+        ))
+    for load, store in pairs:
+        load.start()
+    for load, store in pairs:
+        load.wait()
+        store.start()
+    for load, store in pairs:
+        store.wait()
+
+
 def square_grid(inverse, panel, pattern, dinv):
     width = inverse.shape[3]
     sub, ncols = panel.shape[2], panel.shape[3]
-    vmem = pl.BlockSpec(memory_space=pltpu.VMEM)
+    hbm = pl.BlockSpec(memory_space=pltpu.HBM)
     dma = pltpu.SemaphoreType.DMA
     f32 = jnp.float32
     off, diagonal = pl.pallas_call(
         kernel,
         out_shape=(jax.ShapeDtypeStruct((sub, ncols), f32), jax.ShapeDtypeStruct(dinv.shape, f32)),
-        in_specs=[pl.BlockSpec(memory_space=pltpu.HBM)] * 4,
-        out_specs=(vmem, vmem),
+        in_specs=[hbm] * 4,
+        out_specs=(hbm, hbm),
         scratch_shapes=[
             pltpu.SMEM(pattern.shape, pattern.dtype),
             pltpu.VMEM((width, width), f32),
             pltpu.VMEM(dinv.shape, f32),
             dma((4,)),
+            dma((2,)),
             pltpu.VMEM((GRID, width, width), f32),
             pltpu.VMEM((GRID * width, width), f32),
             pltpu.VMEM((width, width), f32),
@@ -390,6 +426,13 @@
         compiler_params=pltpu.CompilerParams(
             collective_id=0, has_side_effects=True, vmem_limit_bytes=56 * 1024 * 1024),
     )(pattern, inverse.reshape(inverse.shape[2:]), panel.reshape(panel.shape[2:]), dinv)
+    off, diagonal = pl.pallas_call(
+        hand_over,
+        out_shape=(jax.ShapeDtypeStruct(off.shape, f32), jax.ShapeDtypeStruct(dinv.shape, f32)),
+        in_specs=[hbm] * 2,
+        out_specs=(hbm, hbm),
+        scratch_shapes=[pltpu.VMEM(off.shape, f32), pltpu.VMEM(dinv.shape, f32), dma((2, PIECES)), dma((2,))],
+    )(off, diagonal)
     return off.reshape(panel.shape), diagonal
 
 

time: 41.6 us -> 38.8 us (0.933)
  local copies, waits for them, and re-layouts: 2.34 us -> 0 us
    unnamed x4 -> x0, local copies, waits for them, and re-layouts: 2.34 us -> none
    pallas_call x1, Pallas kernels: 38.4 us -> 36.3 us  [square_grid(): pl.pallas_call(kernel, out_shape=(jax.ShapeDtypeStruct((sub, ncols), f32)...]
    pallas_call x0 -> x1, Pallas kernels: none -> 1.71 us  [square_grid(): pl.pallas_call(hand_over, out_shape=(jax.ShapeDtypeStruct(off.shape, f32)...]
where the time goes in v4:
time: 38.8 us; the launch traced here: 38.6 us
  Pallas kernels  38 us (98%)
  between operations  0.64 us (2%)
    pallas_call x1, Pallas kernels, square_grid(): pl.pallas_call(kernel, out_shape=(jax.ShapeDtypeStruct((sub, ncols), f32)...  36.3 us
    pallas_call x1, Pallas kernels, square_grid(): pl.pallas_call(hand_over, out_shape=(jax.ShapeDtypeStruct(off.shape, f32)...  1.71 us

profile of v4, /device:TPU:0, one launch (start us, length us, event | category | flops | bytes accessed | tf_op | source)
XLA Modules:
  0.0 38.6 jit_solution(1967713478763096376)
XLA Ops:
  0.6 36.3 %shard_map.59 = (f32[64,1024]{1,0:T(8,128)}, f32[4,32,128]{2,1,0:T(8,128)}) custom-call(s32[4,4]{1,0:T(4,128)} %pattern_hbm.1, f32[256,256]{1,0:T(8,128)} %bitcast.3, f32[64,1024]{1,0:T(8,128)} %bitcast.4, f32[4,32,128]{2,1,0:T(8,128)} %dinv_hbm.1), custom_call_target="tpu_custom_call" | custom-call | tf_op jit(solution)/shard_map/pallas_call | solution.py:404
  36.9 1.7 %shard_map.60 = (f32[64,1024]{1,0:T(8,128)}, f32[4,32,128]{2,1,0:T(8,128)}) custom-call(f32[64,1024]{1,0:T(8,128)} %get-tuple-element.6.off_in, f32[4,32,128]{2,1,0:T(8,128)} %get-tuple-element.7.diag_in), custom_call_target="tpu_custom_call" | custom-call | tf_op jit(solution)/shard_map/pallas_call | solution.py:429

commit v5 on v4

--- a/solution.py
+++ b/solution.py
@@ -142,12 +142,10 @@
 RELAY_AT = (
     {(1, 0): one(0), (1, 1): one(0) + both(range(CHUNKS)), (1, 2): one(0), (0, 0): both(range(CHUNKS))},
     {},
-    {(1, 2): one(1), (1, 3): one(0)},
-    {(0, 2): one(1)},
-    {(1, 0): both((0,)), (0, 1): both((0,))},
-    {(1, 0): both((1,)), (0, 1): both((1,))},
-    {(1, 0): both((2,)), (0, 1): both((2,))},
-    {(1, 0): both((3,)), (0, 1): both((3,))},
+    {(1, 3): one(0)},
+    {(0, 2): one(1), (1, 2): one(1)},
+    {(1, 0): both(range(CHUNKS)), (0, 1): both(range(CHUNKS))},
+    {}, {}, {},
 )
 
 
@@ -160,14 +158,14 @@
     return out
 
 
-def kernel(pattern_hbm, a_hbm, p_hbm, dinv_hbm, off_ref, diag_ref,
-           pattern_ref, a_ref, dinv_ref, l_sem, w_sem, abuf, pbuf, acc, stage, dpart, dbuf, ebuf, dfin,
+def kernel(pattern_hbm, a_hbm, p_hbm, off_ref, diag_ref,
+           pattern_ref, a_ref, l_sem, w_sem, abuf, pbuf, acc, xacc, stage, dpart, dbuf, ebuf,
            a_send, a_recv, p_send, p_recv, f_send, g_send, o_send, o_recv,
            d_send, d_recv, e_send, e_recv):
     width = a_hbm.shape[0]
     sub = p_hbm.shape[0]
     slab = width // CHUNKS
-    half_u, half_v = dinv_ref.shape[1], dinv_ref.shape[2]
+    half_u, half_v = diag_ref.shape[1], diag_ref.shape[2]
     pole = lax.axis_index("pole")
     row = lax.axis_index("row")
     c = lax.axis_index("col")
@@ -199,7 +197,6 @@
         pltpu.make_async_copy(pattern_hbm, pattern_ref, l_sem.at[0]),
         pltpu.make_async_copy(p_hbm.at[:, cols(z)], pbuf.at[part(q, z), :], l_sem.at[1]),
         pltpu.make_async_copy(a_hbm, a_ref, l_sem.at[2]),
-        pltpu.make_async_copy(dinv_hbm, dinv_ref, l_sem.at[3]),
     ]
     for cp in loads:
         cp.start()
@@ -305,7 +302,31 @@
         return lax.dot_general(left, right, (((0,), (0,)), ((), ())), precision=HIGHEST,
                                preferred_element_type=jnp.float32)
 
-    acc[...] = dot_t(a_ref[...], lhat(z))
+    term_copies = [
+        copy_to(dpart.at[(q + d) % GRID], dbuf.at[d - 1], d_send.at[d], d_recv.at[d - 1], dev(z, (q + d) % GRID))
+        for d in (2, 1, 3)]
+
+    def send_terms():
+        own = lhat(q)
+        terms = dot_t(own, xacc[...]) + dot_t(xacc[...], own)
+        for zt in range(GRID):
+            for qt in range(GRID):
+                u, v = zt * sub + (qt // 2) * half_u, (qt % 2) * half_v
+                dpart[qt, zt] = terms[u:u + half_u, v:v + half_v]
+        for cp in term_copies:
+            cp.start()
+
+    first = dot_t(a_ref[...], lhat(z))
+    acc[...] = first
+
+    @pl.when(q == z)
+    def _():
+        xacc[...] = 0.5 * first
+
+    @pl.when(q != z)
+    def _():
+        xacc[...] = jnp.zeros_like(first)
+
     for step in range(3):
         a_arrive(step)
         slot = slots[step]
@@ -318,7 +339,26 @@
 
         @pl.when(jnp.logical_not(turned))
         def _():
-            acc[...] += jnp.dot(abuf[slot], lhat(slot), precision=HIGHEST, preferred_element_type=jnp.float32)
+            more = jnp.dot(abuf[slot], lhat(slot), precision=HIGHEST, preferred_element_type=jnp.float32)
+            acc[...] += more
+
+            @pl.when(slot == q)
+            def _():
+                xacc[...] += 0.5 * more
+
+            @pl.when(slot != q)
+            def _():
+                xacc[...] += more
+
+        if step < 2:
+            @pl.when(qf == 3 - step)
+            def _():
+                send_terms()
+
+
+    @pl.when(qf < 2)
+    def _():
+        send_terms()
 
     product = acc[...]
     stage[...] = -(product * pattern_ref[q, z].astype(jnp.float32))
@@ -328,16 +368,7 @@
         cp = copy_to(stage.at[part(0, zt), :], off_ref.at[:, cols(z)], o_send.at[d], o_recv.at[z], dev(zt, q))
         cp.start()
         out_copies.append(cp)
-    terms = dot_t(lhat(q), product)
-    for zt in range(GRID):
-        for qt in range(GRID):
-            u, v = zt * sub + (qt // 2) * half_u, (qt % 2) * half_v
-            dpart[qt, zt] = terms[u:u + half_u, v:v + half_v]
-    for d in (2, 1, 3):
-        qt = (q + d) % GRID
-        cp = copy_to(dpart.at[qt], dbuf.at[d - 1], d_send.at[d], d_recv.at[d - 1], dev(z, qt))
-        cp.start()
-        out_copies.append(cp)
+    out_copies += term_copies
     writes = [pltpu.make_async_copy(stage.at[part(0, z), :], off_ref.at[:, cols(z)], w_sem.at[0])]
     writes[0].start()
     total = dpart[q]
@@ -347,16 +378,14 @@
     ebuf[...] = total
     for d in (1, 3, 2):
         zt = (z + d) % GRID
-        cp = copy_to(ebuf.at[zt], dfin.at[z], e_send.at[d], e_recv.at[z], dev(zt, q))
+        cp = copy_to(ebuf.at[zt], diag_ref.at[z], e_send.at[d], e_recv.at[z], dev(zt, q))
         cp.start()
         out_copies.append(cp)
-    dinv_ref[z] = dinv_ref[z] + ebuf[z]
+    writes.append(pltpu.make_async_copy(ebuf.at[z], diag_ref.at[z], w_sem.at[1]))
+    writes[1].start()
     for d in (1, 3, 2):
         k = (z + d) % GRID
-        pltpu.make_async_copy(dfin.at[k], dfin.at[k], e_recv.at[k]).wait()
-        dinv_ref[k] = dinv_ref[k] + dfin[k]
-    writes.append(pltpu.make_async_copy(dinv_ref, diag_ref, w_sem.at[1]))
-    writes[1].start()
+        pltpu.make_async_copy(diag_ref.at[k], diag_ref.at[k], e_recv.at[k]).wait()
     for d in (1, 3, 2):
         zs = (z + d) % GRID
         ref = off_ref.at[:, cols(zs)]
@@ -374,7 +403,7 @@
                         a_copy(a_ref, n, tz, tq, slot, chunk).wait_send()
 
 
-def hand_over(off_in, diag_in, off_out, diag_out, off_held, diag_held, off_sem, diag_sem):
+def hand_over(off_in, diag_in, dinv_in, off_out, diag_out, off_held, diag_held, dinv_held, off_sem, diag_sem):
     rows = off_in.shape[0] // PIECES
     pairs = [(
         pltpu.make_async_copy(diag_in, diag_held, diag_sem.at[0]),
@@ -386,10 +415,15 @@
             pltpu.make_async_copy(off_in.at[piece, :], off_held.at[piece, :], off_sem.at[0, n]),
             pltpu.make_async_copy(off_held.at[piece, :], off_out.at[piece, :], off_sem.at[1, n]),
         ))
+    dinv_load = pltpu.make_async_copy(dinv_in, dinv_held, diag_sem.at[2])
+    dinv_load.start()
     for load, store in pairs:
         load.start()
-    for load, store in pairs:
+    dinv_load.wait()
+    for n, (load, store) in enumerate(pairs):
         load.wait()
+        if n == 0:
+            diag_held[...] += dinv_held[...]
         store.start()
     for load, store in pairs:
         store.wait()
@@ -404,35 +438,35 @@
     off, diagonal = pl.pallas_call(
         kernel,
         out_shape=(jax.ShapeDtypeStruct((sub, ncols), f32), jax.ShapeDtypeStruct(dinv.shape, f32)),
-        in_specs=[hbm] * 4,
+        in_specs=[hbm] * 3,
         out_specs=(hbm, hbm),
         scratch_shapes=[
             pltpu.SMEM(pattern.shape, pattern.dtype),
             pltpu.VMEM((width, width), f32),
-            pltpu.VMEM(dinv.shape, f32),
-            dma((4,)),
+            dma((3,)),
             dma((2,)),
             pltpu.VMEM((GRID, width, width), f32),
             pltpu.VMEM((GRID * width, width), f32),
             pltpu.VMEM((width, width), f32),
             pltpu.VMEM((width, width), f32),
+            pltpu.VMEM((width, width), f32),
             pltpu.VMEM((GRID,) + dinv.shape, f32),
             pltpu.VMEM((GRID - 1,) + dinv.shape, f32),
-            pltpu.VMEM(dinv.shape, f32),
             pltpu.VMEM(dinv.shape, f32),
             dma((8 * CHUNKS,)), dma((GRID * CHUNKS,)), dma((GRID,)), dma((GRID * GRID,)), dma((2 * GRID,)), dma((GRID,)),
             dma((GRID,)), dma((GRID,)), dma((GRID,)), dma((GRID,)), dma((GRID,)), dma((GRID,)),
         ],
         compiler_params=pltpu.CompilerParams(
             collective_id=0, has_side_effects=True, vmem_limit_bytes=56 * 1024 * 1024),
-    )(pattern, inverse.reshape(inverse.shape[2:]), panel.reshape(panel.shape[2:]), dinv)
+    )(pattern, inverse.reshape(inverse.shape[2:]), panel.reshape(panel.shape[2:]))
     off, diagonal = pl.pallas_call(
         hand_over,
         out_shape=(jax.ShapeDtypeStruct(off.shape, f32), jax.ShapeDtypeStruct(dinv.shape, f32)),
-        in_specs=[hbm] * 2,
+        in_specs=[hbm] * 3,
         out_specs=(hbm, hbm),
-        scratch_shapes=[pltpu.VMEM(off.shape, f32), pltpu.VMEM(dinv.shape, f32), dma((2, PIECES)), dma((2,))],
-    )(off, diagonal)
+        scratch_shapes=[pltpu.VMEM(off.shape, f32), pltpu.VMEM(dinv.shape, f32), pltpu.VMEM(dinv.shape, f32),
+                        dma((2, PIECES)), dma((3,))],
+    )(off, diagonal, dinv)
     return off.reshape(panel.shape), diagonal
 
 

time: 38.8 us -> 38.1 us (0.982)
  Pallas kernels: 38 us -> 37.3 us
    pallas_call x1, Pallas kernels: 36.3 us -> 35.6 us  [square_grid(): pl.pallas_call(kernel, out_shape=(jax.ShapeDtypeStruct((sub, ncols), f32)...]
where the time goes in v5:
time: 38.1 us; the launch traced here: 38 us
  Pallas kernels  37.3 us (98%)
  between operations  0.64 us (2%)
    pallas_call x1, Pallas kernels, square_grid(): pl.pallas_call(kernel, out_shape=(jax.ShapeDtypeStruct((sub, ncols), f32)...  35.6 us
    pallas_call x1, Pallas kernels, square_grid(): pl.pallas_call(hand_over, out_shape=(jax.ShapeDtypeStruct(off.shape, f32)...  1.76 us

profile of v5, /device:TPU:0, one launch (start us, length us, event | category | flops | bytes accessed | tf_op | source)
XLA Modules:
  0.0 38.0 jit_solution(1819275137102925204)
XLA Ops:
  0.6 35.6 %shard_map.59 = (f32[64,1024]{1,0:T(8,128)}, f32[4,32,128]{2,1,0:T(8,128)}) custom-call(s32[4,4]{1,0:T(4,128)} %pattern_hbm.1, f32[256,256]{1,0:T(8,128)} %bitcast.3, f32[64,1024]{1,0:T(8,128)} %bitcast.4), custom_call_target="tpu_custom_call" | custom-call | tf_op jit(solution)/shard_map/pallas_call | solution.py:438
  36.2 1.8 %shard_map.60 = (f32[64,1024]{1,0:T(8,128)}, f32[4,32,128]{2,1,0:T(8,128)}) custom-call(f32[64,1024]{1,0:T(8,128)} %get-tuple-element.6.off_in, f32[4,32,128]{2,1,0:T(8,128)} %get-tuple-element.7.diag_in, f32[4,32,128]{2,1,0:T(8,128)} %dinv_in.1), custom_call_target="tpu_custom_call" | custom-call | tf_op jit(solution)/shard_map/pallas_call | solution.py:462

commit v6 on v5

--- a/solution.py
+++ b/solution.py
@@ -308,7 +308,8 @@
 
     def send_terms():
         own = lhat(q)
-        terms = dot_t(own, xacc[...]) + dot_t(xacc[...], own)
+        terms = dot_t(own, xacc[...])
+        terms = terms + terms.T
         for zt in range(GRID):
             for qt in range(GRID):
                 u, v = zt * sub + (qt // 2) * half_u, (qt % 2) * half_v

time: 38.1 us -> 37.9 us (level)
  no operation moved by 1% of the time
where the time goes in v6:
time: 37.9 us; the launch traced here: 37.7 us
  Pallas kernels  37.1 us (98%)
  between operations  0.64 us (2%)
    pallas_call x1, Pallas kernels, square_grid(): pl.pallas_call(kernel, out_shape=(jax.ShapeDtypeStruct((sub, ncols), f32)...  35.3 us
    pallas_call x1, Pallas kernels, square_grid(): pl.pallas_call(hand_over, out_shape=(jax.ShapeDtypeStruct(off.shape, f32)...  1.76 us

profile of v6, /device:TPU:0, one launch (start us, length us, event | category | flops | bytes accessed | tf_op | source)
XLA Modules:
  0.0 37.7 jit_solution(7939082709804850405)
XLA Ops:
  0.6 35.3 %shard_map.59 = (f32[64,1024]{1,0:T(8,128)}, f32[4,32,128]{2,1,0:T(8,128)}) custom-call(s32[4,4]{1,0:T(4,128)} %pattern_hbm.1, f32[256,256]{1,0:T(8,128)} %bitcast.3, f32[64,1024]{1,0:T(8,128)} %bitcast.4), custom_call_target="tpu_custom_call" | custom-call | tf_op jit(solution)/shard_map/pallas_call | solution.py:439
  36.0 1.8 %shard_map.60 = (f32[64,1024]{1,0:T(8,128)}, f32[4,32,128]{2,1,0:T(8,128)}) custom-call(f32[64,1024]{1,0:T(8,128)} %get-tuple-element.6.off_in, f32[4,32,128]{2,1,0:T(8,128)} %get-tuple-element.7.diag_in, f32[4,32,128]{2,1,0:T(8,128)} %dinv_in.1), custom_call_target="tpu_custom_call" | custom-call | tf_op jit(solution)/shard_map/pallas_call | solution.py:463
